TPU v7x, 32 devices: a whole 2x2x4 slice. The times are simulated.
32 devices in a mesh: row: 8 (over z, x), layer: 4 (over y, core).
Axes of the slice: x: 2, y: 2, z: 4, core: 2. Of those that a mesh axis runs over, the one named last changes fastest.
Arguments:
- window_points: int32 [2, 8192], P(None, 'row'), may hold values from 0 to 63
- pivot_points: int32 [2, 512], replicated, may hold values from 0 to 63
- window_factor: bfloat16 [8192, 16384], P('row', 'layer'), may hold values from -1.5 to 1.5
- pivot_factor: bfloat16 [512, 16384], P('row', 'layer'), may hold values from -0.0234375 to 0.0234375
- right_sides: bfloat16 [8192, 512], P('row', 'layer'), may hold values from -6 to 6
- pivot_sides: bfloat16 [512, 512], P('row', 'layer'), may hold values from -6 to 6
Outputs:
- panel_factor: float32 [8192, 512], P('row', 'layer')
- eliminated: float32 [8192, 512], P('row', 'layer')
All inputs are finite; a program needn't handle non-finite values.
Results may differ from a plain program's by a relative error of at most 0.0006.
Values may be sent and summed in bfloat16 or wider, within the bound.
A program may use at most 64 MiB of HBM per device.

v0:
```python
import jax
import jax.numpy as jnp
from jax import lax
from jax.sharding import PartitionSpec as P

nugget_value = 2.0
variance_value = 4.0
length_scale = 4.0


def matern(first_points, second_points):
    first_float = first_points.astype(jnp.float32)
    second_float = second_points.astype(jnp.float32)
    delta_x = first_float[0][:, None] - second_float[0][None, :]
    delta_y = first_float[1][:, None] - second_float[1][None, :]
    scaled = jnp.sqrt(delta_x * delta_x + delta_y * delta_y) * (jnp.sqrt(3.0) / length_scale)
    return variance_value * (1.0 + scaled) * jnp.exp(-scaled)


def solvers(factor):

    def right_solve(matrix):
        return jax.scipy.linalg.solve_triangular(factor, matrix.T, lower=True).T

    def left_solve(matrix):
        return jax.scipy.linalg.solve_triangular(factor, matrix, lower=True)

    return (right_solve, left_solve)


def shards(window_points, pivot_points, window_factor, pivot_factor, right_sides, pivot_sides):
    pivots, pivot_block = (
        lax.all_gather(pivot_factor, "row", axis=0, tiled=True),
        lax.all_gather(pivot_sides, "row", axis=0, tiled=True),
    )
    contract = (((1,), (1,)), ((), ()))
    partial_value = lax.dot_general(
        window_factor, pivots, contract, preferred_element_type=jnp.float32
    )
    gram_part = lax.dot_general(pivots, pivots, contract, preferred_element_type=jnp.float32)
    count = pivots.shape[0]
    cov_diagonal = matern(pivot_points, pivot_points) + nugget_value * jnp.eye(
        count, dtype=jnp.float32
    )
    layers = lax.axis_size("layer")
    layer_index = lax.axis_index("layer")
    rows_here = window_factor.shape[0] // layers
    own_points = lax.dynamic_slice_in_dim(window_points, layer_index * rows_here, rows_here, 1)
    cov_rows = matern(own_points, pivot_points)
    schur_part = lax.psum_scatter(partial_value, "layer", scatter_dimension=0, tiled=True)
    gram_sum = lax.psum(gram_part.astype(jnp.bfloat16), "layer").astype(jnp.float32)
    all_sides = lax.all_gather(pivot_block, "layer", axis=1, tiled=True)
    factor = jnp.linalg.cholesky(cov_diagonal - gram_sum)
    right_solve, left_solve = solvers(factor)
    solved_rows = right_solve(cov_rows - schur_part)
    reduced = left_solve(all_sides.astype(jnp.float32))
    update_rows = jnp.dot(solved_rows, reduced, precision=lax.Precision.HIGHEST)
    panel_out, update = (
        lax.all_to_all(solved_rows, "layer", split_axis=1, concat_axis=0, tiled=True),
        lax.all_to_all(update_rows, "layer", split_axis=1, concat_axis=0, tiled=True),
    )
    eliminated = right_sides.astype(jnp.float32) - update
    return (panel_out, eliminated)


def solution(mesh):
    placed = (
        P(None, "row"),
        P(),
        P("row", "layer"),
        P("row", "layer"),
        P("row", "layer"),
        P("row", "layer"),
    )
    return jax.shard_map(
        shards,
        mesh=mesh,
        in_specs=placed,
        out_specs=(P("row", "layer"), P("row", "layer")),
        check_vma=False,
    )
```

profile of v0, /device:TPU:0, one launch (start us, length us, event | category | flops | bytes accessed | tf_op | source)
XLA Modules:
  0.0 316.1 jit_solution(15572307361402902112)
XLA Ops:
  8.6 33.1 %all_gather.10 = bf16[512,128]{1,0:T(8,128)(2,1)S(1)} all-gather(bf16[64,128]{1,0:T(8,128)(2,1)} %param.11), channel_id=1, replica_groups=mesh['row'=8,'layer'=4] {'row'}, dimensions={0}, use_global_device_ids=true | all-gather | bytes 147456 | tf_op jit(solution)/shard_map/all_gather | solution.py:34
  41.8 7.0 %all_gather.11 = bf16[512,512]{1,0:T(8,128)(2,1)S(1)} all-gather(bf16[512,128]{1,0:T(8,128)(2,1)S(1)} %all_gather.10), channel_id=1, replica_groups=mesh['row'=8,'layer'=4] {'layer'}, dimensions={1}, use_global_device_ids=true | all-gather | bytes 655360 | tf_op jit(solution)/shard_map/all_gather | solution.py:52
  51.0 36.0 %all-gather.2.cloned.1.call-done = bf16[512,4096]{1,0:T(8,128)(2,1)} async-done(((bf16[64,4096]{1,0:T(8,128)(2,1)}), bf16[512,4096]{1,0:T(8,128)(2,1)}) %all-gather.2.cloned.1.call-update) | async-done | bytes 4194320 | tf_op jit(solution)/shard_map/all_gather | solution.py:33
  87.0 6.6 %convolution_convert_fusion = bf16[512,512]{0,1:T(8,128)(2,1)} fusion(bf16[512,4096]{1,0:T(8,128)(2,1)} %all-gather.2.cloned.1.call-done), kind=kOutput, calls=%fused_computation.2 | convolution fusion | flops 2147745792 | bytes 4718592 | tf_op jit(solution)/shard_map/dot_general | solution.py:40
  93.8 10.5 %fusion.59 = f32[1024,512]{1,0:T(8,128)} fusion(bf16[1024,4096]{1,0:T(8,128)(2,1)} %param.8, bf16[512,4096]{1,0:T(8,128)(2,1)} %all-gather.2.cloned.1.call-done), kind=kOutput, calls=%fused_computation.106 | convolution fusion | flops 4294967296 | bytes 14680064 | tf_op jit(solution)/shard_map/dot_general | solution.py:37
  104.4 20.9 %all-reduce.3.cloned.1.call-done = bf16[512,512]{0,1:T(8,128)(2,1)} async-done(((bf16[512,512]{0,1:T(8,128)(2,1)}), bf16[512,512]{0,1:T(8,128)(2,1)}) %all-reduce.3.cloned.1.call-update) | async-done | bytes 524304 | tf_op jit(solution)/shard_map/psum | solution.py:51
  125.2 1.9 convert_subtract_fusion
  127.4 1.9 fusion.7
  129.4 11.7 %cholesky.103 = f32[128,128]{1,0:T(8,128)S(1)} custom-call(f32[128,128]{1,0:T(8,128)S(1)} %cholesky.263), custom_call_target="Cholesky" | custom-call | tf_op jit(solution)/shard_map/jit(cholesky)/cholesky | solution.py:53
  142.4 9.8 %custom-call.34 = f32[1,128,128]{1,2,0:T(8,128)S(1)} custom-call(f32[1,128,128]{2,1,0:T(8,128)S(1)} %get-tuple-element.33), custom_call_target="InvertDiagBlocksLowerTriangular" | custom-call | tf_op jit(solution)/shard_map/jit(cholesky)/cholesky | solution.py:53
  153.4 11.7 %cholesky.215 = f32[128,128]{1,0:T(8,128)S(1)} custom-call(f32[128,128]{1,0:T(8,128)S(1)} %cholesky.267), custom_call_target="Cholesky" | custom-call | tf_op jit(solution)/shard_map/jit(cholesky)/cholesky | solution.py:53
  166.4 10.4 %custom-call.35 = f32[1,128,128]{1,2,0:T(8,128)} custom-call(f32[1,128,128]{2,1,0:T(8,128)S(1)} %get-tuple-element.31), custom_call_target="InvertDiagBlocksLowerTriangular" | custom-call | tf_op jit(solution)/shard_map/jit(cholesky)/cholesky | solution.py:53
  178.6 1.2 convolution_dynamic-update-slice_fusion
  180.4 11.7 %cholesky.236 = f32[128,128]{1,0:T(8,128)S(1)} custom-call(f32[128,128]{1,0:T(8,128)S(1)} %cholesky.272), custom_call_target="Cholesky" | custom-call | tf_op jit(solution)/shard_map/jit(cholesky)/cholesky | solution.py:53
  192.3 10.0 %custom-call.36 = f32[1,128,128]{1,2,0:T(8,128)S(1)} custom-call(f32[1,128,128]{2,1,0:T(8,128)S(1)} %get-tuple-element.29), custom_call_target="InvertDiagBlocksLowerTriangular" | custom-call | tf_op jit(solution)/shard_map/jit(cholesky)/cholesky | solution.py:53
  203.0 11.7 %cholesky.253 = f32[128,128]{1,0:T(8,128)S(1)} custom-call(f32[128,128]{1,0:T(8,128)S(1)} %convolution_subtract_fusion.8), custom_call_target="Cholesky" | custom-call | tf_op jit(solution)/shard_map/jit(cholesky)/cholesky | solution.py:53
  214.9 1.3 compare_reduce_fusion.2
  220.8 10.5 %while.1 = (s32[]{:T(128)}, f32[512,512]{0,1:T(8,128)S(1)}, s32[4,2]{0,1:T(2,128)S(1)}, f32[4,128,128]{2,1,0:T(8,128)}, s32[]{:T(128)}) while((s32[]{:T(128)}, f32[512,512]{0,1:T(8,128)S(1)}, s32[4,2]{0,1:T(2,128)S(1)}, f32[4,128,128]{2,1,0:T(8,128)}, s32[]{:T(128)}) %tuple.31), condition=%wide.while_cond, body=%wide.while_body.sunk | while | flops 2 | bytes 393329 | solution.py:23
  221.3 1.3 dynamic-slice.7
  224.0 1.3 dynamic-slice.7
  226.6 1.3 dynamic-slice.7
  229.2 1.3 dynamic-slice.7
  231.3 40.1 %custom-call.37 = f32[4,128,128]{1,2,0:T(8,128)S(1)} custom-call(f32[4,128,128]{2,1,0:T(8,128)} %get-tuple-element.9), custom_call_target="InvertDiagBlocksLowerTriangular" | custom-call | tf_op jit(solution)/shard_map/jit(_solve_triangular)/triangular_solve | solution.py:23
  271.4 1.3 fusion.30
  275.2 1.5 subtract_bitcast_fusion
  284.0 3.5 %all-to-all-start = ((f32[256,4,128]{0,2,1:T(8,128)}), f32[256,4,128]{0,2,1:T(8,128)S(1)}, u32[]{:S(2)}, u32[]{:S(2)}) async-start(f32[256,4,128]{0,2,1:T(8,128)} %bitcast.79), calls=%async_computation.1 | async-start | bytes 1048576 | tf_op jit(solution)/shard_map/all_to_all | solution.py:59
  287.5 1.6 convolution_subtract_fusion.2
  289.1 1.3 fusion.47
  290.4 2.1 convolution_bitcast_fusion
  293.3 2.9 all-to-all-done
  296.3 3.5 %all-to-all-start.1 = ((f32[256,4,128]{2,0,1:T(8,128)}), f32[256,4,128]{2,0,1:T(8,128)S(1)}, u32[]{:S(2)}, u32[]{:S(2)}) async-start(f32[256,4,128]{2,0,1:T(8,128)} %bitcast.71), calls=%async_computation.2 | async-start | bytes 1048576 | tf_op jit(solution)/shard_map/all_to_all | solution.py:60
  300.7 7.8 %all-to-all-done.1 = f32[256,4,128]{2,0,1:T(8,128)S(1)} async-done(((f32[256,4,128]{2,0,1:T(8,128)}), f32[256,4,128]{2,0,1:T(8,128)S(1)}, u32[]{:S(2)}, u32[]{:S(2)}) %all-to-all-start.1) | async-done | bytes 524320 | tf_op jit(solution)/shard_map/all_to_all | solution.py:60
  (80 shorter events, 31.0 us)
Async XLA Ops:
  7.2 79.8 %all-gather.2.cloned.1.call-start = ((), (), s32[]{:S(2)}) async-start(), calls=%async_computation.3 | async-start | bytes 4718592 | tf_op jit(solution)/shard_map/all_gather | solution.py:33
  7.9 117.3 %all-reduce.3.cloned.1.call-start = ((), (), s32[]{:S(2)}) async-start(), calls=%async_computation.4 | async-start | bytes 1048576 | tf_op jit(solution)/shard_map/psum | solution.py:51
  48.8 0.8 copy-start
  93.6 181.6 %reduce-scatter.2.cloned.1.call-start = ((), (), s32[]{:S(2)}) async-start(), calls=%async_computation.5 | async-start | bytes 2621440 | tf_op jit(solution)/shard_map/reduce_scatter | solution.py:50
  271.4 3.8 %copy-start.1 = (f32[4,128,128]{1,2,0:T(8,128)}, f32[4,128,128]{1,2,0:T(8,128)S(1)}, u32[]{:S(2)}) copy-start(f32[4,128,128]{1,2,0:T(8,128)S(1)} %custom-call.37) | copy-start | bytes 786436
  283.1 0.8 copy-start.2
  284.0 12.3 %all-to-all-start = ((f32[256,4,128]{0,2,1:T(8,128)}), f32[256,4,128]{0,2,1:T(8,128)S(1)}, u32[]{:S(2)}, u32[]{:S(2)}) async-start(f32[256,4,128]{0,2,1:T(8,128)} %bitcast.79), calls=%async_computation.1 | async-start | bytes 1048576 | tf_op jit(solution)/shard_map/all_to_all | solution.py:59
  289.1 19.5 %copy-start.3 = (bf16[1024,128]{1,0:T(8,128)(2,1)S(1)}, bf16[1024,128]{1,0:T(8,128)(2,1)}, u32[]{:S(2)}) copy-start(bf16[1024,128]{1,0:T(8,128)(2,1)} %param.10) | copy-start | bytes 786436
  296.3 12.3 %all-to-all-start.1 = ((f32[256,4,128]{2,0,1:T(8,128)}), f32[256,4,128]{2,0,1:T(8,128)S(1)}, u32[]{:S(2)}, u32[]{:S(2)}) async-start(f32[256,4,128]{2,0,1:T(8,128)} %bitcast.71), calls=%async_computation.2 | async-start | bytes 1048576 | tf_op jit(solution)/shard_map/all_to_all | solution.py:60
Sparse Core Ops, SparseCore 0:
  10.1 76.7 all-gather.1
  93.7 31.4 all-reduce.2
  127.8 31.4 reduce-scatter.1
where the time goes:
time: 320 us; the launch traced here: 316 us
  other arithmetic  130 us (41%)
  waiting for transfers between devices  68.3 us (21%)
  blocking collectives  40.1 us (13%)
  matrix products  35.9 us (11%)
  local copies, waits for them, and re-layouts  17.7 us (6%)
  between operations  16.8 us (5%)
  starting transfers between devices  7.24 us (2%)
    another operation x14, other arithmetic, shards(): factor = jnp.linalg.cholesky(cov_diagonal - gram_sum)  80.7 us
    another operation x4, other arithmetic, right_solve(): return jax.scipy.linalg.solve_triangular(factor, matrix.T, lower=True).T  41.6 us
    all_gather x1, waiting for transfers between devices, shards(): lax.all_gather(pivot_factor, 'row', axis=0, tiled=True)  36 us
    all_gather x1, blocking collectives, shards(): lax.all_gather(pivot_sides, 'row', axis=0, tiled=True)  33.1 us
    psum x1, waiting for transfers between devices, shards(): lax.psum(gram_part.astype(jnp.bfloat16), 'layer').astype(jnp.float32)  20.9 us
    dot_general x1, matrix products, shards(): lax.dot_general(window_factor, pivots, contract, preferred_element_type=j...  10.5 us
    another operation x20, local copies, waits for them, and re-layouts  10.5 us
    all_to_all x1, waiting for transfers between devices, shards(): lax.all_to_all(update_rows, 'layer', split_axis=1, concat_axis=0, tiled=T...  7.82 us
  transfers between devices with their start and end apart: 5, of which 4 were waited for; matrix products, arithmetic and copies ran while one was open for 53% of the time, Pallas kernels for 0%

commit v1 on v0

--- a/solution.py
+++ b/solution.py
@@ -1,6 +1,8 @@
 import jax
 import jax.numpy as jnp
 from jax import lax
+from jax.experimental import pallas as pl
+from jax.experimental.pallas import tpu as pltpu
 from jax.sharding import PartitionSpec as P
 
 nugget_value = 2.0
@@ -17,15 +19,102 @@
     return variance_value * (1.0 + scaled) * jnp.exp(-scaled)
 
 
-def solvers(factor):
+lanes = 128
+tile_rows = 8
+group = 4
+highest = lax.Precision.HIGHEST
 
-    def right_solve(matrix):
-        return jax.scipy.linalg.solve_triangular(factor, matrix.T, lower=True).T
 
-    def left_solve(matrix):
-        return jax.scipy.linalg.solve_triangular(factor, matrix, lower=True)
+def invert_tile(read_tile, write_row):
+    shape = (tile_rows, lanes)
+    count = lanes // tile_rows
+    row_of = lax.broadcasted_iota(jnp.int32, shape, 0)
+    lane_of = lax.broadcasted_iota(jnp.int32, shape, 1)
+    block = [read_tile(t) for t in range(count)]
+    extra = [jnp.where(row_of + t * tile_rows == lane_of, 1.0, 0.0) for t in range(count)]
+    for first in range(0, lanes, group):
+        top, low = first // tile_rows, first % tile_rows
+        live = range(top, count)
+        columns = [
+            {t: jnp.broadcast_to(block[t][:, first + k : first + k + 1], shape) for t in live}
+            for k in range(group)
+        ]
 
-    return (right_solve, left_solve)
+        def spread(tile, k):
+            return jnp.broadcast_to(tile[low + k : low + k + 1, :], shape)
+
+        rows = [spread(block[top], k) for k in range(group)]
+        ends = [spread(extra[top], k) for k in range(group)]
+        for k in range(group):
+            pivot = spread(columns[k][top], k)
+            inverse = 1.0 / pivot
+            write_row(first + k, (ends[k] * lax.rsqrt(pivot))[0:1, :])
+            for m in range(k + 1, group):
+                factor = spread(columns[k][top], m) * inverse
+                rows[m] = rows[m] - factor * rows[k]
+                ends[m] = ends[m] - factor * ends[k]
+                for t in live:
+                    columns[m][t] = columns[m][t] - columns[k][t] * factor
+            rows[k] = rows[k] * inverse
+            ends[k] = ends[k] * inverse
+        for t in live:
+            if t == top and low + group == tile_rows:
+                continue
+            for k in range(group):
+                weight = columns[k][t]
+                if t == top:
+                    weight = jnp.where(row_of >= low + group, weight, 0.0)
+                block[t] = block[t] - weight * rows[k]
+                extra[t] = extra[t] - weight * ends[k]
+
+
+def inverse_kernel(matrix_ref, out_ref, work_ref, tile_ref):
+    size = matrix_ref.shape[0]
+    work_ref[:, :size] = matrix_ref[...]
+    row_of = lax.broadcasted_iota(jnp.int32, (size, size), 0)
+    lane_of = lax.broadcasted_iota(jnp.int32, (size, size), 1)
+    work_ref[:, size:] = jnp.where(row_of == lane_of, 1.0, 0.0)
+
+    def step(index, carry):
+        start = pl.multiple_of(index * lanes, lanes)
+
+        def read_tile(t):
+            return work_ref[pl.ds(start + t * tile_rows, tile_rows), pl.ds(start, lanes)]
+
+        def write_row(at, value):
+            tile_ref[at : at + 1, :] = value
+
+        invert_tile(read_tile, write_row)
+        solved = jnp.dot(
+            tile_ref[...],
+            work_ref[pl.ds(start, lanes), :],
+            precision=highest,
+            preferred_element_type=jnp.float32,
+        )
+        out_ref[pl.ds(start, lanes), :] = solved[:, size:]
+        below = lax.broadcasted_iota(jnp.int32, (lanes, size), 1) >= start + lanes
+        left = jnp.where(below, solved[:, :size], 0.0)
+        work_ref[...] -= jnp.dot(
+            left.T, solved, precision=highest, preferred_element_type=jnp.float32
+        )
+        return carry
+
+    lax.fori_loop(0, size // lanes, step, 0)
+
+
+def inverse_factor(matrix):
+    size = matrix.shape[0]
+    return pl.pallas_call(
+        inverse_kernel,
+        out_shape=jax.ShapeDtypeStruct((size, size), jnp.float32),
+        in_specs=[pl.BlockSpec(memory_space=pltpu.VMEM)],
+        out_specs=pl.BlockSpec(memory_space=pltpu.VMEM),
+        scratch_shapes=[
+            pltpu.VMEM((size, 2 * size), jnp.float32),
+            pltpu.VMEM((lanes, lanes), jnp.float32),
+        ],
+        compiler_params=pltpu.CompilerParams(vmem_limit_bytes=32 * 1024 * 1024),
+    )(matrix)
 
 
 def shards(window_points, pivot_points, window_factor, pivot_factor, right_sides, pivot_sides):
@@ -50,15 +139,15 @@
     schur_part = lax.psum_scatter(partial_value, "layer", scatter_dimension=0, tiled=True)
     gram_sum = lax.psum(gram_part.astype(jnp.bfloat16), "layer").astype(jnp.float32)
     all_sides = lax.all_gather(pivot_block, "layer", axis=1, tiled=True)
-    factor = jnp.linalg.cholesky(cov_diagonal - gram_sum)
-    right_solve, left_solve = solvers(factor)
-    solved_rows = right_solve(cov_rows - schur_part)
-    reduced = left_solve(all_sides.astype(jnp.float32))
-    update_rows = jnp.dot(solved_rows, reduced, precision=lax.Precision.HIGHEST)
-    panel_out, update = (
-        lax.all_to_all(solved_rows, "layer", split_axis=1, concat_axis=0, tiled=True),
-        lax.all_to_all(update_rows, "layer", split_axis=1, concat_axis=0, tiled=True),
+    inverse = inverse_factor(cov_diagonal - gram_sum)
+    solved_rows = lax.dot_general(
+        cov_rows - schur_part, inverse, contract, precision=highest
     )
+    reduced = jnp.dot(inverse, all_sides.astype(jnp.float32), precision=highest)
+    update_rows = jnp.dot(solved_rows, reduced, precision=highest)
+    both = jnp.stack([solved_rows, update_rows])
+    moved = lax.all_to_all(both, "layer", split_axis=2, concat_axis=1, tiled=True)
+    panel_out, update = moved[0], moved[1]
     eliminated = right_sides.astype(jnp.float32) - update
     return (panel_out, eliminated)
 

time: 320 us -> 208 us (0.65); the launches traced: 316 us -> 208 us
  other arithmetic: 130 us -> 3.46 us
  Pallas kernels: 0 us -> 32.3 us
  local copies, waits for them, and re-layouts: 17.7 us -> 2.78 us
  blocking collectives: 40.1 us -> 54.7 us
  matrix products: 35.9 us -> 21.6 us
  waiting for transfers between devices: 68.3 us -> 79.1 us
  starting transfers between devices: 7.24 us -> 0.12 us
    another operation x18 -> x1, other arithmetic: 122 us -> 0.07 us  [shards(): both = jnp.stack([solved_rows, update_rows])]
    all_gather x1, waiting for transfers between devices: 36 us -> 78.3 us  [shards(): lax.all_gather(pivot_factor, 'row', axis=0, tiled=True)]
    pallas_call x0 -> x1, Pallas kernels: none -> 32.3 us  [inverse_factor(): pl.pallas_call(inverse_kernel, out_shape=jax.ShapeDtypeStruct((size, size...]
    psum x1, waiting for transfers between devices: 20.9 us -> 0.02 us  [shards(): lax.psum(gram_part.astype(jnp.bfloat16), 'layer').astype(jnp.float32)]
    all_to_all x0 -> x1, blocking collectives: none -> 16.9 us  [shards(): lax.all_to_all(both, 'layer', split_axis=2, concat_axis=1, tiled=True)]
    another operation x20 -> x0, matrix products: 16.7 us -> none  [the longest x7 6.66 us: left_solve(): return jax.scipy.linalg.solve_triangular(factor, matrix, lower=True)]
    another operation x34 -> x1, local copies, waits for them, and re-layouts: 14.8 us -> 0.58 us  [shards(): both = jnp.stack([solved_rows, update_rows])]
    all_to_all x2 -> x0, waiting for transfers between devices: 10.8 us -> none  [the longest x1 7.82 us: shards(): lax.all_to_all(update_rows, 'layer', split_axis=1, concat_axis=0, tiled=T...]
  transfers between devices with their start and end apart: 5 -> 3, of which waited for: 4 -> 1; matrix products, arithmetic and copies ran while one was open for 53% -> 7% of each run, Pallas kernels for 0% -> 16%
where the time goes in v1:
time: 208 us
  waiting for transfers between devices  79.1 us (38%)
  blocking collectives  54.7 us (26%)
  Pallas kernels  32.3 us (16%)
  matrix products  21.6 us (10%)
  between operations  13.9 us (7%)
  other arithmetic  3.46 us (2%)
  local copies, waits for them, and re-layouts  2.78 us (1%)
    all_gather x1, waiting for transfers between devices, shards(): lax.all_gather(pivot_factor, 'row', axis=0, tiled=True)  78.3 us
    pallas_call x1, Pallas kernels, inverse_factor(): pl.pallas_call(inverse_kernel, out_shape=jax.ShapeDtypeStruct((size, size...  32.3 us
    all_gather x1, blocking collectives, shards(): lax.all_gather(pivot_sides, 'row', axis=0, tiled=True)  30.5 us
    all_to_all x1, blocking collectives, shards(): lax.all_to_all(both, 'layer', split_axis=2, concat_axis=1, tiled=True)  16.9 us
    dot_general x1, matrix products, shards(): lax.dot_general(window_factor, pivots, contract, preferred_element_type=j...  10.5 us
    all_gather x1, blocking collectives, shards(): all_sides = lax.all_gather(pivot_block, 'layer', axis=1, tiled=True)  7.33 us
    dot_general x1, matrix products, shards(): lax.dot_general(pivots, pivots, contract, preferred_element_type=jnp.floa...  6.62 us
  transfers between devices with their start and end apart: 3, of which 1 were waited for; matrix products, arithmetic and copies ran while one was open for 7% of the time, Pallas kernels for 16%

profile of v1, /device:TPU:0, one launch (start us, length us, event | category | flops | bytes accessed | tf_op | source)
XLA Modules:
  0.0 208.0 jit_solution(16860491836559513668)
XLA Ops:
  7.2 0.0 all-gather.2.cloned.1.call-start
  7.2 0.7 all-gather.2.cloned.1.call-update
  7.9 0.0 all-reduce.2.cloned.1.call-start
  7.9 78.3 %all-gather.2.cloned.1.call-done = bf16[512,4096]{1,0:T(8,128)(2,1)} async-done(((bf16[64,4096]{1,0:T(8,128)(2,1)}), bf16[512,4096]{1,0:T(8,128)(2,1)}) %all-gather.2.cloned.1.call-update) | async-done | bytes 4194320 | tf_op jit(solution)/shard_map/all_gather | solution.py:122
  86.2 6.6 %convolution_convert_fusion = bf16[512,512]{1,0:T(8,128)(2,1)} fusion(bf16[512,4096]{1,0:T(8,128)(2,1)} %all-gather.2.cloned.1.call-done), kind=kOutput, calls=%fused_computation | convolution fusion | flops 2147745792 | bytes 4718592 | tf_op jit(solution)/shard_map/dot_general | solution.py:129
  92.9 0.0 all-reduce.2.cloned.1.call-update
  92.9 0.0 copy-start.2
  92.9 0.0 copy-start.1
  92.9 0.0 reduce-scatter.2.cloned.1.call-start
  93.0 10.5 %fusion.27 = f32[1024,512]{1,0:T(8,128)} fusion(bf16[1024,4096]{1,0:T(8,128)(2,1)} %param.8, bf16[512,4096]{1,0:T(8,128)(2,1)} %all-gather.2.cloned.1.call-done), kind=kOutput, calls=%fused_computation.34 | convolution fusion | flops 4294967296 | bytes 14680064 | tf_op jit(solution)/shard_map/dot_general | solution.py:126
  103.5 0.0 reduce-scatter.2.cloned.1.call-update
  103.5 0.0 copy-done.2
  103.5 0.0 copy-done.1
  103.5 30.5 %all_gather.10 = bf16[512,128]{1,0:T(8,128)(2,1)S(1)} all-gather(bf16[64,128]{1,0:T(8,128)(2,1)S(1)} %copy-done.1), channel_id=1, replica_groups=mesh['row'=8,'layer'=4] {'row'}, dimensions={0}, use_global_device_ids=true | all-gather | bytes 147456 | tf_op jit(solution)/shard_map/all_gather | solution.py:123
  134.1 0.7 dynamic-slice_convert_fusion
  134.8 7.3 %all_gather.11 = bf16[512,512]{1,0:T(8,128)(2,1)S(1)} all-gather(bf16[512,128]{1,0:T(8,128)(2,1)S(1)} %all_gather.10), channel_id=1, replica_groups=mesh['row'=8,'layer'=4] {'layer'}, dimensions={1}, use_global_device_ids=true | all-gather | bytes 655360 | tf_op jit(solution)/shard_map/all_gather | solution.py:141
  142.1 0.0 all-reduce.2.cloned.1.call-done
  142.1 1.9 convert_subtract_fusion.matrix_ref
  144.0 32.3 %shard_map.77 = f32[512,512]{1,0:T(8,128)S(1)} custom-call(f32[512,512]{1,0:T(8,128)S(1)} %convert_subtract_fusion.matrix_ref), custom_call_target="tpu_custom_call" | custom-call | tf_op jit(solution)/shard_map/pallas_call | solution.py:107
  176.3 1.0 fusion.28
  177.3 0.0 reduce-scatter.2.cloned.1.call-done
  177.3 2.5 %fusion = f32[256,512]{1,0:T(8,128)S(1)} fusion(f32[512,512]{1,0:T(8,128)S(1)} %shard_map.77, f32[256,512]{1,0:T(8,128)} %reduce-scatter.2.cloned.1.call-done, f32[512]{0:T(512)S(1)} %bitcast.28, f32[256]{0:T(256)S(1)} %bitcast.30, f32[512]{0:T(512)S(1)} %bitcast.26, f32[256]{0:T(256)S(1)} %bitcast.29), kind=kOutput, calls=%fused_computation.6 | convolution fusion | flops 806748160 | bytes 2103296 | tf_op jit(solution)/shard_map/dot_general | solution.py:143
  179.8 1.1 convolution_bitcast_fusion
  180.8 0.1 pad_maximum_fusion
  180.9 0.0 copy-start
  180.9 0.6 copy.10
  181.5 16.9 %all_to_all.15 = f32[2,256,512]{1,0,2:T(2,128)S(1)} all-to-all(f32[2,256,512]{1,0,2:T(2,128)S(1)} %copy.10), channel_id=1, replica_groups=mesh['row'=8,'layer'=4] {'layer'}, dimensions={2} | all-to-all | bytes 2097152 | tf_op jit(solution)/shard_map/all_to_all | solution.py:149
  198.4 0.8 fusion.24
  199.2 1.0 copy.11
  200.3 0.3 copy.12
  200.6 0.0 copy-done
  200.6 0.8 bitcast_subtract_fusion
  (3 shorter events, 0.0 us)
Async XLA Ops:
  7.2 79.1 %all-gather.2.cloned.1.call-start = ((), (), s32[]{:S(2)}) async-start(), calls=%async_computation.2 | async-start | bytes 4718592 | tf_op jit(solution)/shard_map/all_gather | solution.py:122
  7.9 134.2 %all-reduce.2.cloned.1.call-start = ((), (), s32[]{:S(2)}) async-start(), calls=%async_computation.4 | async-start | bytes 1048576 | tf_op jit(solution)/shard_map/psum | solution.py:140
  92.9 10.6 %copy-start.2 = (s32[2,512]{1,0:T(2,128)S(1)}, s32[2,512]{1,0:T(2,128)}, u32[]{:S(2)}) copy-start(s32[2,512]{1,0:T(2,128)} %param.7) | copy-start | bytes 12292
  92.9 10.6 %copy-start.1 = (bf16[64,128]{1,0:T(8,128)(2,1)S(1)}, bf16[64,128]{1,0:T(8,128)(2,1)}, u32[]{:S(2)}) copy-start(bf16[64,128]{1,0:T(8,128)(2,1)} %param.11) | copy-start | bytes 49156
  92.9 84.4 %reduce-scatter.2.cloned.1.call-start = ((), (), s32[]{:S(2)}) async-start(), calls=%async_computation.3 | async-start | bytes 2621440 | tf_op jit(solution)/shard_map/reduce_scatter | solution.py:139
  180.9 19.7 %copy-start = (bf16[1024,128]{1,0:T(8,128)(2,1)S(1)}, bf16[1024,128]{1,0:T(8,128)(2,1)}, u32[]{:S(2)}) copy-start(bf16[1024,128]{1,0:T(8,128)(2,1)} %param.10) | copy-start | bytes 786436
Sparse Core Ops, SparseCore 0:
  10.1 76.0 all-gather.1
  93.0 31.4 all-reduce.1
  127.1 31.4 reduce-scatter.1

commit v2 on v1

--- a/solution.py
+++ b/solution.py
@@ -1,3 +1,5 @@
+import functools
+
 import jax
 import jax.numpy as jnp
 from jax import lax
@@ -117,11 +119,152 @@
     )(matrix)
 
 
+def remote(src, dst, send, recv, axis, target):
+    return pltpu.make_async_remote_copy(
+        src_ref=src,
+        dst_ref=dst,
+        send_sem=send,
+        recv_sem=recv,
+        device_id={axis: target},
+        device_id_type=pl.DeviceIdType.MESH,
+    )
+
+
+def greet(axis, targets):
+    barrier = pltpu.get_barrier_semaphore()
+    for target in targets:
+        pl.semaphore_signal(
+            barrier, inc=1, device_id={axis: target}, device_id_type=pl.DeviceIdType.MESH
+        )
+    pl.semaphore_wait(barrier, len(targets))
+
+
+def gather_kernel(axis, count, split, block_ref, out_ref, send_sem, recv_sem):
+    me = lax.axis_index(axis)
+    odd = me % 2
+    place = (1 - odd) * (me // 2) + odd * (count - 1 - me // 2)
+
+    def member(spot):
+        spot = (spot + count) % count
+        upper = spot // (count // 2)
+        return (1 - upper) * (2 * spot) + upper * (2 * (count - 1 - spot) + 1)
+
+    right, left = member(place + 1), member(place - 1)
+    greet(axis, (left, right))
+    copies = []
+    for step in range(count - 1):
+        for way, target, part in ((0, right, pl.ds(0, split)), (1, left, pl.ds(split, block_ref.shape[1] - split))):
+            owner = member(place - step) if way == 0 else member(place + step)
+            source = block_ref.at[:, part] if step == 0 else out_ref.at[owner, :, part]
+            copy = remote(
+                source,
+                out_ref.at[owner, :, part],
+                send_sem.at[way, step],
+                recv_sem.at[way, step],
+                axis,
+                target,
+            )
+            if step > 0:
+                copies[2 * (step - 1) + way].wait_recv()
+            copy.start()
+            copies.append(copy)
+        if step == 0:
+            out_ref[me] = block_ref[...]
+    for copy in copies[-2:]:
+        copy.wait_recv()
+    for copy in copies:
+        copy.wait_send()
+
+
+def gather_rows(block, axis):
+    count = lax.axis_size(axis)
+    rows, columns = block.shape
+    split = columns // 256 * 128
+    vmem = pl.BlockSpec(memory_space=pltpu.VMEM)
+    return pl.pallas_call(
+        functools.partial(gather_kernel, axis, count, split),
+        out_shape=jax.ShapeDtypeStruct((count, rows, columns), block.dtype),
+        in_specs=[vmem],
+        out_specs=vmem,
+        scratch_shapes=[
+            pltpu.SemaphoreType.DMA((2, count - 1)),
+            pltpu.SemaphoreType.DMA((2, count - 1)),
+        ],
+        compiler_params=pltpu.CompilerParams(
+            collective_id=0, has_side_effects=True, vmem_limit_bytes=32 * 1024 * 1024
+        ),
+    )(block)
+
+
+def sum_kernel(axis, count, part_ref, sides_ref, total_ref, all_ref, out_buf, in_buf, send_sem, recv_sem):
+    me = lax.axis_index(axis)
+    rounds = count.bit_length() - 1
+    greet(axis, [(me + shift) % count for shift in range(1, count)])
+    copies = []
+    for level in range(rounds):
+        bit = 1 << level
+        partner = me + (1 - 2 * ((me // bit) % 2)) * bit
+        source = part_ref if level == 0 else out_buf.at[level]
+        copy = remote(
+            source, in_buf.at[level], send_sem.at[level], recv_sem.at[level], axis, partner
+        )
+        copy.start()
+        if level == 0:
+            for shift in range(1, count):
+                spot = rounds + shift - 1
+                copies.append(
+                    remote(
+                        sides_ref,
+                        all_ref.at[me],
+                        send_sem.at[spot],
+                        recv_sem.at[spot],
+                        axis,
+                        (me + shift) % count,
+                    )
+                )
+                copies[-1].start()
+            all_ref[me] = sides_ref[...]
+        copy.wait()
+        total = source[...].astype(jnp.float32) + in_buf[level].astype(jnp.float32)
+        if level + 1 < rounds:
+            out_buf[level + 1] = total.astype(out_buf.dtype)
+        else:
+            total_ref[...] = total
+    for copy in copies:
+        copy.wait()
+
+
+def sum_parts(part, sides, axis):
+    count = lax.axis_size(axis)
+    rounds = count.bit_length() - 1
+    copies = rounds + count - 1
+    vmem = pl.BlockSpec(memory_space=pltpu.VMEM)
+    return pl.pallas_call(
+        functools.partial(sum_kernel, axis, count),
+        out_shape=(
+            jax.ShapeDtypeStruct(part.shape, jnp.float32),
+            jax.ShapeDtypeStruct((count,) + sides.shape, sides.dtype),
+        ),
+        in_specs=[vmem, vmem],
+        out_specs=(vmem, vmem),
+        scratch_shapes=[
+            pltpu.VMEM((rounds,) + part.shape, part.dtype),
+            pltpu.VMEM((rounds,) + part.shape, part.dtype),
+            pltpu.SemaphoreType.DMA((copies,)),
+            pltpu.SemaphoreType.DMA((copies,)),
+        ],
+        compiler_params=pltpu.CompilerParams(
+            collective_id=1, has_side_effects=True, vmem_limit_bytes=32 * 1024 * 1024
+        ),
+    )(part, sides)
+
+
 def shards(window_points, pivot_points, window_factor, pivot_factor, right_sides, pivot_sides):
-    pivots, pivot_block = (
-        lax.all_gather(pivot_factor, "row", axis=0, tiled=True),
-        lax.all_gather(pivot_sides, "row", axis=0, tiled=True),
-    )
+    depth, width = pivot_factor.shape[1], pivot_sides.shape[1]
+    padded = jnp.pad(pivot_sides, ((0, 0), (0, -width % lanes)))
+    gathered = gather_rows(jnp.concatenate([pivot_factor, padded], axis=1), "row")
+    gathered = gathered.reshape(-1, gathered.shape[2])
+    pivots, pivot_block = gathered[:, :depth], gathered[:, depth : depth + width]
     contract = (((1,), (1,)), ((), ()))
     partial_value = lax.dot_general(
         window_factor, pivots, contract, preferred_element_type=jnp.float32
@@ -137,8 +280,8 @@
     own_points = lax.dynamic_slice_in_dim(window_points, layer_index * rows_here, rows_here, 1)
     cov_rows = matern(own_points, pivot_points)
     schur_part = lax.psum_scatter(partial_value, "layer", scatter_dimension=0, tiled=True)
-    gram_sum = lax.psum(gram_part.astype(jnp.bfloat16), "layer").astype(jnp.float32)
-    all_sides = lax.all_gather(pivot_block, "layer", axis=1, tiled=True)
+    gram_sum, all_parts = sum_parts(gram_part.astype(jnp.bfloat16), pivot_block, "layer")
+    all_sides = jnp.swapaxes(all_parts, 0, 1).reshape(count, layers * width)
     inverse = inverse_factor(cov_diagonal - gram_sum)
     solved_rows = lax.dot_general(
         cov_rows - schur_part, inverse, contract, precision=highest

time: 208 us -> 177 us (0.85)
  Pallas kernels: 32.3 us -> 115 us
  waiting for transfers between devices: 79.1 us -> 0.04 us
  blocking collectives: 54.7 us -> 17.7 us
  local copies, waits for them, and re-layouts: 2.78 us -> 5.9 us
    pallas_call x0 -> x2, Pallas kernels: none -> 82.7 us  [the longest x1 53 us: gather_rows(): pl.pallas_call(functools.partial(gather_kernel, axis, count, split), out_...]
    all_gather x1 -> x0, waiting for transfers between devices: 78.3 us -> none  [shards(): lax.all_gather(pivot_factor, 'row', axis=0, tiled=True)]
    all_gather x2 -> x0, blocking collectives: 37.9 us -> none  [the longest x1 30.5 us: shards(): lax.all_gather(pivot_sides, 'row', axis=0, tiled=True)]
    dot_general x1, matrix products: 10.5 us -> 8.37 us  [shards(): lax.dot_general(window_factor, pivots, contract, preferred_element_type=j...]
  transfers between devices with their start and end apart: 3 -> 1, of which waited for: 1 -> 0; matrix products, arithmetic and copies ran while one was open for 7% -> 6% of each run, Pallas kernels for 16% -> 35%
where the time goes in v2:
time: 177 us; the launch traced here: 176 us
  Pallas kernels  115 us (65%)
  matrix products  19.8 us (11%)
  blocking collectives  17.7 us (10%)
  between operations  14.2 us (8%)
  local copies, waits for them, and re-layouts  5.9 us (3%)
  other arithmetic  3.48 us (2%)
    pallas_call x1, Pallas kernels, gather_rows(): pl.pallas_call(functools.partial(gather_kernel, axis, count, split), out_...  53 us
    pallas_call x1, Pallas kernels, inverse_factor(): pl.pallas_call(inverse_kernel, out_shape=jax.ShapeDtypeStruct((size, size...  32.5 us
    pallas_call x1, Pallas kernels, sum_parts(): pl.pallas_call(functools.partial(sum_kernel, axis, count), out_shape=(jax...  29.7 us
    all_to_all x1, blocking collectives, shards(): lax.all_to_all(both, 'layer', split_axis=2, concat_axis=1, tiled=True)  17.7 us
    dot_general x1, matrix products, shards(): lax.dot_general(window_factor, pivots, contract, preferred_element_type=j...  8.37 us
    dot_general x1, matrix products, shards(): lax.dot_general(pivots, pivots, contract, preferred_element_type=jnp.floa...  6.13 us
  transfers between devices with their start and end apart: 1, of which 0 were waited for; matrix products, arithmetic and copies ran while one was open for 6% of the time, Pallas kernels for 35%

profile of v2, /device:TPU:0, one launch (start us, length us, event | category | flops | bytes accessed | tf_op | source)
XLA Modules:
  0.0 176.3 jit_solution(4853040030683783487)
XLA Ops:
  7.2 0.0 reduce-scatter.2.cloned.1.call-start
  7.2 1.1 pad_maximum_fusion.1.block_ref
  8.3 53.0 %shard_map.77 = bf16[8,64,4224]{2,1,0:T(8,128)(2,1)S(1)} custom-call(bf16[64,4224]{1,0:T(8,128)(2,1)S(1)} %pad_maximum_fusion.1.block_ref), custom_call_target="tpu_custom_call" | custom-call | tf_op jit(solution)/shard_map/pallas_call | solution.py:184
  61.3 0.0 copy-start
  61.3 2.0 %copy-done = bf16[8,64,4224]{2,1,0:T(8,128)(2,1)} copy-done((bf16[8,64,4224]{2,1,0:T(8,128)(2,1)}, bf16[8,64,4224]{2,1,0:T(8,128)(2,1)S(1)}, u32[]{:S(2)}) %copy-start) | copy-done | bytes 4325400
  63.3 0.0 copy-start.2
  63.3 8.4 %fusion.4 = f32[1024,512]{0,1:T(8,128)} fusion(bf16[1024,4096]{1,0:T(8,128)(2,1)} %param.8, bf16[512,4224]{1,0:T(8,128)(2,1)S(1)} %bitcast.24), kind=kOutput, calls=%fused_computation.4 | convolution fusion | flops 4294967296 | bytes 14680064 | tf_op jit(solution)/shard_map/dot_general | solution.py:269
  71.7 0.0 reduce-scatter.2.cloned.1.call-update
  71.7 0.9 slice.43.sides_ref
  72.7 0.0 copy-done.2
  72.7 6.1 %fusion.7.part_ref = bf16[512,512]{1,0:T(8,128)(2,1)S(1)} fusion(bf16[512,4224]{1,0:T(8,128)(2,1)} %bitcast.26), kind=kOutput, calls=%fused_computation.5 | convolution fusion | flops 2147745792 | bytes 4718592 | tf_op jit(solution)/shard_map/dot_general | solution.py:272
  78.8 29.7 %shard_map.78 = (f32[512,512]{1,0:T(8,128)S(1)}, bf16[4,512,128]{2,1,0:T(8,128)(2,1)S(1)}) custom-call(bf16[512,512]{1,0:T(8,128)(2,1)S(1)} %fusion.7.part_ref, bf16[512,128]{1,0:T(8,128)(2,1)S(1)} %slice.43.sides_ref), custom_call_target="tpu_custom_call" | custom-call | tf_op jit(solution)/shard_map/pallas_call | solution.py:242
  108.5 0.8 add_subtract_fusion.matrix_ref
  109.3 32.5 %shard_map.79 = f32[512,512]{1,0:T(8,128)S(1)} custom-call(f32[512,512]{1,0:T(8,128)S(1)} %add_subtract_fusion.matrix_ref), custom_call_target="tpu_custom_call" | custom-call | tf_op jit(solution)/shard_map/pallas_call | solution.py:109
  141.8 0.2 copy.13
  142.0 0.7 dynamic-slice_convert_fusion
  142.7 1.0 fusion.37
  143.7 0.0 reduce-scatter.2.cloned.1.call-done
  143.8 3.2 %fusion.10 = f32[256,512]{1,0:T(8,128)S(1)} fusion(f32[512,512]{1,0:T(8,128)S(1)} %shard_map.79, f32[256,512]{0,1:T(8,128)} %reduce-scatter.2.cloned.1.call-done, f32[512]{0:T(512)S(1)} %bitcast.35, f32[256]{0:T(256)S(1)} %bitcast.37, f32[512]{0:T(512)S(1)} %bitcast.33, f32[256]{0:T(256)S(1)} %bitcast.36), kind=kOutput, calls=%fused_computation.12 | convolution fusion | flops 806748160 | bytes 2103296 | tf_op jit(solution)/shard_map/dot_general | solution.py:286
  147.0 1.1 convolution_bitcast_fusion
  148.0 0.1 pad_maximum_fusion
  148.1 0.0 copy-start.1
  148.1 0.6 copy.14
  148.7 17.7 %all_to_all.15 = f32[2,256,512]{1,0,2:T(2,128)S(1)} all-to-all(f32[2,256,512]{1,0,2:T(2,128)S(1)} %copy.14), channel_id=1, replica_groups=mesh['row'=8,'layer'=4] {'layer'}, dimensions={2} | all-to-all | bytes 2097152 | tf_op jit(solution)/shard_map/all_to_all | solution.py:292
  166.4 0.8 fusion.34
  167.2 0.3 copy.16
  167.6 1.0 copy.15
  168.6 0.0 copy-done.1
  168.6 0.8 bitcast_subtract_fusion
  (3 shorter events, 0.0 us)
Async XLA Ops:
  7.2 136.6 %reduce-scatter.2.cloned.1.call-start = ((), (), s32[]{:S(2)}) async-start(), calls=%async_computation.2 | async-start | bytes 2621440 | tf_op jit(solution)/shard_map/reduce_scatter | solution.py:282
  61.3 2.0 %copy-start = (bf16[8,64,4224]{2,1,0:T(8,128)(2,1)}, bf16[8,64,4224]{2,1,0:T(8,128)(2,1)S(1)}, u32[]{:S(2)}) copy-start(bf16[8,64,4224]{2,1,0:T(8,128)(2,1)S(1)} %shard_map.77) | copy-start | bytes 12976132
  63.3 9.3 %copy-start.2 = (s32[2,512]{1,0:T(2,128)S(1)}, s32[2,512]{1,0:T(2,128)}, u32[]{:S(2)}) copy-start(s32[2,512]{1,0:T(2,128)} %param.7) | copy-start | bytes 12292
  148.1 20.5 %copy-start.1 = (bf16[1024,128]{1,0:T(8,128)(2,1)S(1)}, bf16[1024,128]{1,0:T(8,128)(2,1)}, u32[]{:S(2)}) copy-start(bf16[1024,128]{1,0:T(8,128)(2,1)} %param.10) | copy-start | bytes 786436
Sparse Core Ops, SparseCore 0:
  71.9 39.2 reduce-scatter.1

commit v3 on v2

--- a/solution.py
+++ b/solution.py
@@ -24,6 +24,7 @@
 lanes = 128
 tile_rows = 8
 group = 4
+ring_parts = 4
 highest = lax.Precision.HIGHEST
 
 
@@ -139,7 +140,7 @@
     pl.semaphore_wait(barrier, len(targets))
 
 
-def gather_kernel(axis, count, split, block_ref, out_ref, send_sem, recv_sem):
+def gather_kernel(axis, count, parts, block_ref, out_ref, send_sem, recv_sem):
     me = lax.axis_index(axis)
     odd = me % 2
     place = (1 - odd) * (me // 2) + odd * (count - 1 - me // 2)
@@ -153,24 +154,26 @@
     greet(axis, (left, right))
     copies = []
     for step in range(count - 1):
-        for way, target, part in ((0, right, pl.ds(0, split)), (1, left, pl.ds(split, block_ref.shape[1] - split))):
+        for lane, (start, stop) in enumerate(parts):
+            way = lane % 2
+            part = pl.ds(start, stop - start)
             owner = member(place - step) if way == 0 else member(place + step)
             source = block_ref.at[:, part] if step == 0 else out_ref.at[owner, :, part]
             copy = remote(
                 source,
                 out_ref.at[owner, :, part],
-                send_sem.at[way, step],
-                recv_sem.at[way, step],
+                send_sem.at[lane, step],
+                recv_sem.at[lane, step],
                 axis,
-                target,
+                right if way == 0 else left,
             )
             if step > 0:
-                copies[2 * (step - 1) + way].wait_recv()
+                copies[len(parts) * (step - 1) + lane].wait_recv()
             copy.start()
             copies.append(copy)
         if step == 0:
             out_ref[me] = block_ref[...]
-    for copy in copies[-2:]:
+    for copy in copies[-len(parts) :]:
         copy.wait_recv()
     for copy in copies:
         copy.wait_send()
@@ -179,16 +182,18 @@
 def gather_rows(block, axis):
     count = lax.axis_size(axis)
     rows, columns = block.shape
-    split = columns // 256 * 128
+    pieces = columns // lanes
+    cuts = [pieces * at // ring_parts * lanes for at in range(ring_parts)] + [columns]
+    parts = tuple(zip(cuts[:-1], cuts[1:]))
     vmem = pl.BlockSpec(memory_space=pltpu.VMEM)
     return pl.pallas_call(
-        functools.partial(gather_kernel, axis, count, split),
+        functools.partial(gather_kernel, axis, count, parts),
         out_shape=jax.ShapeDtypeStruct((count, rows, columns), block.dtype),
         in_specs=[vmem],
         out_specs=vmem,
         scratch_shapes=[
-            pltpu.SemaphoreType.DMA((2, count - 1)),
-            pltpu.SemaphoreType.DMA((2, count - 1)),
+            pltpu.SemaphoreType.DMA((ring_parts, count - 1)),
+            pltpu.SemaphoreType.DMA((ring_parts, count - 1)),
         ],
         compiler_params=pltpu.CompilerParams(
             collective_id=0, has_side_effects=True, vmem_limit_bytes=32 * 1024 * 1024
@@ -259,6 +264,70 @@
     )(part, sides)
 
 
+def finish_kernel(
+    axis, count, rows_ref, inverse_ref, reduced_ref, right_ref, panel_ref, rest_ref,
+    panel_buf, update_buf, land_buf, send_sem, recv_sem
+):
+    me = lax.axis_index(axis)
+    width = panel_ref.shape[2]
+    greet(axis, [(me + shift) % count for shift in range(1, count)])
+    copies = []
+
+    def send(kind, source, target_ref):
+        for shift in range(1, count):
+            target = (me + shift) % count
+            copy = remote(
+                source.at[target],
+                target_ref.at[me],
+                send_sem.at[kind, shift - 1],
+                recv_sem.at[kind, shift - 1],
+                axis,
+                target,
+            )
+            copy.start()
+            copies.append(copy)
+        target_ref[me] = source[me]
+
+    solved = lax.dot_general(
+        rows_ref[...],
+        inverse_ref[...],
+        (((1,), (1,)), ((), ())),
+        precision=highest,
+        preferred_element_type=jnp.float32,
+    )
+    for part in range(count):
+        panel_buf[part] = solved[:, part * width : (part + 1) * width]
+    send(0, panel_buf, panel_ref)
+    update = jnp.dot(
+        solved, reduced_ref[...], precision=highest, preferred_element_type=jnp.float32
+    )
+    for part in range(count):
+        update_buf[part] = update[:, part * width : (part + 1) * width]
+    send(1, update_buf, land_buf)
+    for copy in copies:
+        copy.wait()
+    rest_ref[...] = right_ref[...].astype(jnp.float32) - land_buf[...]
+
+
+def finish(rows, inverse, reduced, right, axis):
+    count = lax.axis_size(axis)
+    shape = (count, rows.shape[0], right.shape[1])
+    vmem = pl.BlockSpec(memory_space=pltpu.VMEM)
+    out = jax.ShapeDtypeStruct(shape, jnp.float32)
+    panel, rest = pl.pallas_call(
+        functools.partial(finish_kernel, axis, count),
+        out_shape=(out, out),
+        in_specs=[vmem] * 4,
+        out_specs=(vmem, vmem),
+        scratch_shapes=[pltpu.VMEM(shape, jnp.float32)] * 3
+        + [pltpu.SemaphoreType.DMA((2, count - 1))] * 2,
+        compiler_params=pltpu.CompilerParams(
+            collective_id=2, has_side_effects=True, vmem_limit_bytes=32 * 1024 * 1024
+        ),
+    )(rows, inverse, reduced, right.reshape(shape))
+    return panel.reshape(right.shape), rest.reshape(right.shape)
+
+
 def shards(window_points, pivot_points, window_factor, pivot_factor, right_sides, pivot_sides):
     depth, width = pivot_factor.shape[1], pivot_sides.shape[1]
     padded = jnp.pad(pivot_sides, ((0, 0), (0, -width % lanes)))
@@ -266,9 +335,6 @@
     gathered = gathered.reshape(-1, gathered.shape[2])
     pivots, pivot_block = gathered[:, :depth], gathered[:, depth : depth + width]
     contract = (((1,), (1,)), ((), ()))
-    partial_value = lax.dot_general(
-        window_factor, pivots, contract, preferred_element_type=jnp.float32
-    )
     gram_part = lax.dot_general(pivots, pivots, contract, preferred_element_type=jnp.float32)
     count = pivots.shape[0]
     cov_diagonal = matern(pivot_points, pivot_points) + nugget_value * jnp.eye(
@@ -279,20 +345,16 @@
     rows_here = window_factor.shape[0] // layers
     own_points = lax.dynamic_slice_in_dim(window_points, layer_index * rows_here, rows_here, 1)
     cov_rows = matern(own_points, pivot_points)
+    gram_sum, all_parts = sum_parts(gram_part.astype(jnp.bfloat16), pivot_block, "layer")
+    gathered, gram_sum = lax.optimization_barrier((gathered, gram_sum))
+    partial_value = lax.dot_general(
+        window_factor, gathered[:, :depth], contract, preferred_element_type=jnp.float32
+    )
     schur_part = lax.psum_scatter(partial_value, "layer", scatter_dimension=0, tiled=True)
-    gram_sum, all_parts = sum_parts(gram_part.astype(jnp.bfloat16), pivot_block, "layer")
     all_sides = jnp.swapaxes(all_parts, 0, 1).reshape(count, layers * width)
     inverse = inverse_factor(cov_diagonal - gram_sum)
-    solved_rows = lax.dot_general(
-        cov_rows - schur_part, inverse, contract, precision=highest
-    )
     reduced = jnp.dot(inverse, all_sides.astype(jnp.float32), precision=highest)
-    update_rows = jnp.dot(solved_rows, reduced, precision=highest)
-    both = jnp.stack([solved_rows, update_rows])
-    moved = lax.all_to_all(both, "layer", split_axis=2, concat_axis=1, tiled=True)
-    panel_out, update = moved[0], moved[1]
-    eliminated = right_sides.astype(jnp.float32) - update
-    return (panel_out, eliminated)
+    return finish(cov_rows - schur_part, inverse, reduced, right_sides, "layer")
 
 
 def solution(mesh):

time: 177 us -> 145 us (0.82)
  blocking collectives: 17.7 us -> 0 us
  matrix products: 19.8 us -> 9.22 us
  local copies, waits for them, and re-layouts: 5.9 us -> 1.85 us
    all_to_all x1 -> x0, blocking collectives: 17.7 us -> none  [shards(): lax.all_to_all(both, 'layer', split_axis=2, concat_axis=1, tiled=True)]
    pallas_call x1, Pallas kernels: 29.7 us -> 20.1 us  [sum_parts(): pl.pallas_call(functools.partial(sum_kernel, axis, count), out_shape=(jax...]
    pallas_call x1 -> x2, Pallas kernels: 53 us -> 62.1 us  [the longest x1 47.5 us: gather_rows(): pl.pallas_call(functools.partial(gather_kernel, axis, count, parts), out_...]
    dot_general x3 -> x1, matrix products: 12.6 us -> 5.85 us  [shards(): lax.dot_general(window_factor, gathered[:, :depth], contract, preferred_e...]
    dot_general x1, matrix products: 6.13 us -> 2.36 us  [shards(): lax.dot_general(pivots, pivots, contract, preferred_element_type=jnp.floa...]
    slice x3 -> x0, local copies, waits for them, and re-layouts: 2.18 us -> none  [shards(): panel_out, update = (moved[0], moved[1])]
  transfers between devices with their start and end apart: 1 -> 1, of which waited for: 0 -> 0; matrix products, arithmetic and copies ran while one was open for 6% -> 2% of each run, Pallas kernels for 35% -> 23%
where the time goes in v3:
time: 145 us; the launch traced here: 144 us
  Pallas kernels  115 us (79%)
  between operations  14.2 us (10%)
  matrix products  9.22 us (6%)
  other arithmetic  4.03 us (3%)
  local copies, waits for them, and re-layouts  1.85 us (1%)
    pallas_call x1, Pallas kernels, gather_rows(): pl.pallas_call(functools.partial(gather_kernel, axis, count, parts), out_...  47.5 us
    pallas_call x1, Pallas kernels, inverse_factor(): pl.pallas_call(inverse_kernel, out_shape=jax.ShapeDtypeStruct((size, size...  32.5 us
    pallas_call x1, Pallas kernels, sum_parts(): pl.pallas_call(functools.partial(sum_kernel, axis, count), out_shape=(jax...  20.1 us
    pallas_call x1, Pallas kernels, finish(): pl.pallas_call(functools.partial(finish_kernel, axis, count), out_shape=(...  14.6 us
    dot_general x1, matrix products, shards(): lax.dot_general(window_factor, gathered[:, :depth], contract, preferred_e...  5.85 us
  transfers between devices with their start and end apart: 1, of which 0 were waited for; matrix products, arithmetic and copies ran while one was open for 2% of the time, Pallas kernels for 23%

profile of v3, /device:TPU:0, one launch (start us, length us, event | category | flops | bytes accessed | tf_op | source)
XLA Modules:
  0.0 144.1 jit_solution(14233476333114418187)
XLA Ops:
  7.2 0.0 reduce-scatter.2.cloned.1.call-start
  7.2 1.1 pad_maximum_fusion.block_ref
  8.3 0.0 slice-start
  8.3 47.5 %shard_map.77 = bf16[8,64,4224]{2,1,0:T(8,128)(2,1)S(1)} custom-call(bf16[64,4224]{1,0:T(8,128)(2,1)S(1)} %pad_maximum_fusion.block_ref), custom_call_target="tpu_custom_call" | custom-call | tf_op jit(solution)/shard_map/pallas_call | solution.py:189
  55.9 0.0 slice-start.1
  55.9 2.4 %fusion.7.part_ref = bf16[512,512]{1,0:T(8,128)(2,1)S(1)} fusion(bf16[512,4224]{1,0:T(8,128)(2,1)S(1)} %bitcast.15), kind=kOutput, calls=%fused_computation.5 | convolution fusion | flops 2147745792 | bytes 4718592 | tf_op jit(solution)/shard_map/dot_general | solution.py:338
  58.3 20.1 %shard_map.78 = (f32[512,512]{1,0:T(8,128)S(1)}, bf16[4,512,128]{2,1,0:T(8,128)(2,1)S(1)}) custom-call(bf16[512,512]{1,0:T(8,128)(2,1)S(1)} %fusion.7.part_ref, bf16[512,128]{1,0:T(8,128)(2,1)S(1)} %slice.37.sides_ref), custom_call_target="tpu_custom_call" | custom-call | tf_op jit(solution)/shard_map/pallas_call | solution.py:247
  78.4 0.0 slice-done
  78.4 0.0 slice-done.1
  78.4 0.0 copy-start.1
  78.4 5.9 %fusion.4 = f32[1024,512]{1,0:T(8,128)} fusion(bf16[1024,4096]{1,0:T(8,128)(2,1)S(1)} %bitcast.30, bf16[512,4224]{1,0:T(8,128)(2,1)S(1)} %bitcast.17), kind=kOutput, calls=%fused_computation.4 | convolution fusion | flops 4294967296 | bytes 14680064 | tf_op jit(solution)/shard_map/dot_general | solution.py:350
  84.3 0.0 reduce-scatter.2.cloned.1.call-update
  84.3 0.0 copy-done.1
  84.4 0.0 copy-start
  84.4 0.8 add_subtract_fusion.matrix_ref
  85.2 32.5 %shard_map.79.inverse_ref = f32[512,512]{1,0:T(8,128)S(1)} custom-call(f32[512,512]{1,0:T(8,128)S(1)} %add_subtract_fusion.matrix_ref), custom_call_target="tpu_custom_call" | custom-call | tf_op jit(solution)/shard_map/pallas_call | solution.py:110
  117.6 0.2 copy.10
  117.8 0.7 dynamic-slice_convert_fusion
  118.5 1.0 fusion.12.reduced_ref
  119.6 0.0 reduce-scatter.2.cloned.1.call-done
  119.6 1.5 %multiply_subtract_fusion.rows_ref = f32[256,512]{1,0:T(8,128)S(1)} fusion(f32[256,512]{1,0:T(8,128)} %reduce-scatter.2.cloned.1.call-done, f32[512]{0:T(512)S(1)} %bitcast.26, f32[256]{0:T(256)S(1)} %bitcast.28, f32[512]{0:T(512)S(1)} %bitcast.24, f32[256]{0:T(256)S(1)} %bitcast.27), kind=kLoop, calls=%fused_computation.9 | loop fusion | flops 1441792 | bytes 1054720 | tf_op jit(solution)/shard_map/sub | solution.py:357
  121.1 0.0 copy-done
  121.1 14.6 %shard_map.80 = (f32[4,256,128]{2,1,0:T(8,128)S(1)}, f32[4,256,128]{2,1,0:T(8,128)S(1)}) custom-call(f32[256,512]{1,0:T(8,128)S(1)} %multiply_subtract_fusion.rows_ref, f32[512,512]{1,0:T(8,128)S(1)} %shard_map.79.inverse_ref, f32[512,512]{1,0:T(8,128)S(1)} %fusion.12.reduced_ref, bf16[4,256,128]{2,1,0:T(8,128)(2,1)S(1)} %bitcast.21), custom_call_target="tpu_custom_call" | custom-call | tf_op jit(solution)/shard_map/pallas_call | solution.py:317
  135.6 0.8 copy.14
  136.4 0.8 copy.15
  (5 shorter events, 0.0 us)
Async XLA Ops:
  7.2 112.4 %reduce-scatter.2.cloned.1.call-start = ((), (), s32[]{:S(2)}) async-start(), calls=%async_computation.1 | async-start | bytes 2621440 | tf_op jit(solution)/shard_map/reduce_scatter | solution.py:353
  8.3 70.1 %slice-start = ((s8[8388608]{0:T(1024)(128)(4,1)}), s8[4194304]{0:T(1024)(128)(4,1)S(1)}, s32[]{:S(2)}) async-start(s8[8388608]{0:T(1024)(128)(4,1)} %bitcast.29), calls=%async_computation.2 | async-start | bytes 8388608
  55.9 22.5 %slice-start.1 = ((s8[8388608]{0:T(1024)(128)(4,1)}), s8[4194304]{0:T(1024)(128)(4,1)S(1)}, s32[]{:S(2)}) async-start(s8[8388608]{0:T(1024)(128)(4,1)} %bitcast.29), calls=%async_computation.3 | async-start | bytes 8388608
  78.4 5.9 %copy-start.1 = (s32[2,512]{1,0:T(2,128)S(1)}, s32[2,512]{1,0:T(2,128)}, u32[]{:S(2)}) copy-start(s32[2,512]{1,0:T(2,128)} %param.7) | copy-start | bytes 12292
  84.4 36.7 %copy-start = (bf16[1024,128]{1,0:T(8,128)(2,1)S(1)}, bf16[1024,128]{1,0:T(8,128)(2,1)}, u32[]{:S(2)}) copy-start(bf16[1024,128]{1,0:T(8,128)(2,1)} %param.10) | copy-start | bytes 786436
Sparse Core Ops, SparseCore 0:
  84.4 31.4 reduce-scatter.1

commit v4 on v3

--- a/solution.py
+++ b/solution.py
@@ -23,7 +23,7 @@
 
 lanes = 128
 tile_rows = 8
-group = 4
+group = 8
 ring_parts = 4
 highest = lax.Precision.HIGHEST
 

time: 145 us -> 141 us (0.972)
  Pallas kernels: 115 us -> 107 us
  waiting for transfers between devices: 0.04 us -> 2.84 us
    pallas_call x1, Pallas kernels: 32.5 us -> 26 us  [inverse_factor(): pl.pallas_call(inverse_kernel, out_shape=jax.ShapeDtypeStruct((size, size...]
    reduce_scatter x1, waiting for transfers between devices: 0.02 us -> 2.82 us  [shards(): lax.psum_scatter(partial_value, 'layer', scatter_dimension=0, tiled=True)]
  transfers between devices with their start and end apart: 1 -> 1, of which waited for: 0 -> 1; matrix products, arithmetic and copies ran while one was open for 2% -> 2% of each run, Pallas kernels for 23% -> 19%
where the time goes in v4:
time: 141 us; the launch traced here: 139 us
  Pallas kernels  107 us (76%)
  between operations  14.2 us (10%)
  matrix products  9.22 us (7%)
  other arithmetic  4.02 us (3%)
  waiting for transfers between devices  2.84 us (2%)
  local copies, waits for them, and re-layouts  1.85 us (1%)
    pallas_call x1, Pallas kernels, gather_rows(): pl.pallas_call(functools.partial(gather_kernel, axis, count, parts), out_...  47.5 us
    pallas_call x1, Pallas kernels, inverse_factor(): pl.pallas_call(inverse_kernel, out_shape=jax.ShapeDtypeStruct((size, size...  26 us
    pallas_call x1, Pallas kernels, sum_parts(): pl.pallas_call(functools.partial(sum_kernel, axis, count), out_shape=(jax...  20.1 us
    pallas_call x1, Pallas kernels, finish(): pl.pallas_call(functools.partial(finish_kernel, axis, count), out_shape=(...  13.4 us
    dot_general x1, matrix products, shards(): lax.dot_general(window_factor, gathered[:, :depth], contract, preferred_e...  5.85 us
    reduce_scatter x1, waiting for transfers between devices, shards(): lax.psum_scatter(partial_value, 'layer', scatter_dimension=0, tiled=True)  2.82 us
  transfers between devices with their start and end apart: 1, of which 1 were waited for; matrix products, arithmetic and copies ran while one was open for 2% of the time, Pallas kernels for 19%

profile of v4, /device:TPU:0, one launch (start us, length us, event | category | flops | bytes accessed | tf_op | source)
XLA Modules:
  0.0 139.2 jit_solution(15604075448219213986)
XLA Ops:
  7.2 0.0 reduce-scatter.2.cloned.1.call-start
  7.2 1.1 pad_maximum_fusion.block_ref
  8.3 0.0 slice-start
  8.3 47.5 %shard_map.77 = bf16[8,64,4224]{2,1,0:T(8,128)(2,1)S(1)} custom-call(bf16[64,4224]{1,0:T(8,128)(2,1)S(1)} %pad_maximum_fusion.block_ref), custom_call_target="tpu_custom_call" | custom-call | tf_op jit(solution)/shard_map/pallas_call | solution.py:189
  55.9 0.0 slice-start.1
  55.9 2.4 %fusion.7.part_ref = bf16[512,512]{1,0:T(8,128)(2,1)S(1)} fusion(bf16[512,4224]{1,0:T(8,128)(2,1)S(1)} %bitcast.15), kind=kOutput, calls=%fused_computation.5 | convolution fusion | flops 2147745792 | bytes 4718592 | tf_op jit(solution)/shard_map/dot_general | solution.py:338
  58.3 20.1 %shard_map.78 = (f32[512,512]{1,0:T(8,128)S(1)}, bf16[4,512,128]{2,1,0:T(8,128)(2,1)S(1)}) custom-call(bf16[512,512]{1,0:T(8,128)(2,1)S(1)} %fusion.7.part_ref, bf16[512,128]{1,0:T(8,128)(2,1)S(1)} %slice.37.sides_ref), custom_call_target="tpu_custom_call" | custom-call | tf_op jit(solution)/shard_map/pallas_call | solution.py:247
  78.4 0.0 slice-done
  78.4 0.0 slice-done.1
  78.4 0.0 copy-start.1
  78.4 5.9 %fusion.4 = f32[1024,512]{1,0:T(8,128)} fusion(bf16[1024,4096]{1,0:T(8,128)(2,1)S(1)} %bitcast.30, bf16[512,4224]{1,0:T(8,128)(2,1)S(1)} %bitcast.17), kind=kOutput, calls=%fused_computation.4 | convolution fusion | flops 4294967296 | bytes 14680064 | tf_op jit(solution)/shard_map/dot_general | solution.py:350
  84.3 0.0 reduce-scatter.2.cloned.1.call-update
  84.3 0.0 copy-done.1
  84.4 0.0 copy-start
  84.4 0.8 add_subtract_fusion.matrix_ref
  85.2 26.0 %shard_map.79.inverse_ref = f32[512,512]{1,0:T(8,128)S(1)} custom-call(f32[512,512]{1,0:T(8,128)S(1)} %add_subtract_fusion.matrix_ref), custom_call_target="tpu_custom_call" | custom-call | tf_op jit(solution)/shard_map/pallas_call | solution.py:110
  111.1 0.2 copy.10
  111.4 0.7 dynamic-slice_convert_fusion
  112.1 1.0 fusion.12.reduced_ref
  113.1 2.8 %reduce-scatter.2.cloned.1.call-done = f32[256,512]{1,0:T(8,128)} async-done(((f32[1024,512]{1,0:T(8,128)}), f32[256,512]{1,0:T(8,128)}) %reduce-scatter.2.cloned.1.call-update) | async-done | bytes 524304 | tf_op jit(solution)/shard_map/reduce_scatter | solution.py:353
  115.9 1.5 %multiply_subtract_fusion.rows_ref = f32[256,512]{1,0:T(8,128)S(1)} fusion(f32[256,512]{1,0:T(8,128)} %reduce-scatter.2.cloned.1.call-done, f32[512]{0:T(512)S(1)} %bitcast.26, f32[256]{0:T(256)S(1)} %bitcast.28, f32[512]{0:T(512)S(1)} %bitcast.24, f32[256]{0:T(256)S(1)} %bitcast.27), kind=kLoop, calls=%fused_computation.9 | loop fusion | flops 1441792 | bytes 1054720 | tf_op jit(solution)/shard_map/sub | solution.py:357
  117.4 0.0 copy-done
  117.4 13.4 %shard_map.80 = (f32[4,256,128]{2,1,0:T(8,128)S(1)}, f32[4,256,128]{2,1,0:T(8,128)S(1)}) custom-call(f32[256,512]{1,0:T(8,128)S(1)} %multiply_subtract_fusion.rows_ref, f32[512,512]{1,0:T(8,128)S(1)} %shard_map.79.inverse_ref, f32[512,512]{1,0:T(8,128)S(1)} %fusion.12.reduced_ref, bf16[4,256,128]{2,1,0:T(8,128)(2,1)S(1)} %bitcast.21), custom_call_target="tpu_custom_call" | custom-call | tf_op jit(solution)/shard_map/pallas_call | solution.py:317
  130.8 0.8 copy.14
  131.6 0.8 copy.15
  (5 shorter events, 0.0 us)
Async XLA Ops:
  7.2 108.7 %reduce-scatter.2.cloned.1.call-start = ((), (), s32[]{:S(2)}) async-start(), calls=%async_computation.1 | async-start | bytes 2621440 | tf_op jit(solution)/shard_map/reduce_scatter | solution.py:353
  8.3 70.1 %slice-start = ((s8[8388608]{0:T(1024)(128)(4,1)}), s8[4194304]{0:T(1024)(128)(4,1)S(1)}, s32[]{:S(2)}) async-start(s8[8388608]{0:T(1024)(128)(4,1)} %bitcast.29), calls=%async_computation.2 | async-start | bytes 8388608
  55.9 22.5 %slice-start.1 = ((s8[8388608]{0:T(1024)(128)(4,1)}), s8[4194304]{0:T(1024)(128)(4,1)S(1)}, s32[]{:S(2)}) async-start(s8[8388608]{0:T(1024)(128)(4,1)} %bitcast.29), calls=%async_computation.3 | async-start | bytes 8388608
  78.4 5.9 %copy-start.1 = (s32[2,512]{1,0:T(2,128)S(1)}, s32[2,512]{1,0:T(2,128)}, u32[]{:S(2)}) copy-start(s32[2,512]{1,0:T(2,128)} %param.7) | copy-start | bytes 12292
  84.4 33.0 %copy-start = (bf16[1024,128]{1,0:T(8,128)(2,1)S(1)}, bf16[1024,128]{1,0:T(8,128)(2,1)}, u32[]{:S(2)}) copy-start(bf16[1024,128]{1,0:T(8,128)(2,1)} %param.10) | copy-start | bytes 786436
Sparse Core Ops, SparseCore 0:
  84.4 31.4 reduce-scatter.1

commit v5 on v4

--- a/solution.py
+++ b/solution.py
@@ -95,11 +95,15 @@
             preferred_element_type=jnp.float32,
         )
         out_ref[pl.ds(start, lanes), :] = solved[:, size:]
-        below = lax.broadcasted_iota(jnp.int32, (lanes, size), 1) >= start + lanes
-        left = jnp.where(below, solved[:, :size], 0.0)
-        work_ref[...] -= jnp.dot(
-            left.T, solved, precision=highest, preferred_element_type=jnp.float32
-        )
+
+        @pl.when(index < size // lanes - 1)
+        def reduce_rest():
+            below = lax.broadcasted_iota(jnp.int32, (lanes, size), 1) >= start + lanes
+            left = jnp.where(below, solved[:, :size], 0.0)
+            work_ref[...] -= jnp.dot(
+                left.T, solved, precision=highest, preferred_element_type=jnp.float32
+            )
+
         return carry
 
     lax.fori_loop(0, size // lanes, step, 0)

time: 141 us -> 141 us (level)
  transfers between devices with their start and end apart: 1 -> 1, of which waited for: 1 -> 1; matrix products, arithmetic and copies ran while one was open for 2% -> 2% of each run, Pallas kernels for 19% -> 18%
where the time goes in v5:
time: 141 us; the launch traced here: 139 us
  Pallas kernels  106 us (75%)
  between operations  14.2 us (10%)
  matrix products  9.23 us (7%)
  other arithmetic  4.03 us (3%)
  waiting for transfers between devices  4.01 us (3%)
  local copies, waits for them, and re-layouts  1.85 us (1%)
    pallas_call x1, Pallas kernels, gather_rows(): pl.pallas_call(functools.partial(gather_kernel, axis, count, parts), out_...  47.5 us
    pallas_call x1, Pallas kernels, inverse_factor(): pl.pallas_call(inverse_kernel, out_shape=jax.ShapeDtypeStruct((size, size...  24.8 us
    pallas_call x1, Pallas kernels, sum_parts(): pl.pallas_call(functools.partial(sum_kernel, axis, count), out_shape=(jax...  20.1 us
    pallas_call x1, Pallas kernels, finish(): pl.pallas_call(functools.partial(finish_kernel, axis, count), out_shape=(...  13.4 us
    dot_general x1, matrix products, shards(): lax.dot_general(window_factor, gathered[:, :depth], contract, preferred_e...  5.85 us
    reduce_scatter x1, waiting for transfers between devices, shards(): lax.psum_scatter(partial_value, 'layer', scatter_dimension=0, tiled=True)  4 us
  transfers between devices with their start and end apart: 1, of which 1 were waited for; matrix products, arithmetic and copies ran while one was open for 2% of the time, Pallas kernels for 18%

profile of v5, /device:TPU:0, one launch (start us, length us, event | category | flops | bytes accessed | tf_op | source)
XLA Modules:
  0.0 139.2 jit_solution(17820528163477106372)
XLA Ops:
  7.2 0.0 reduce-scatter.2.cloned.1.call-start
  7.2 1.1 pad_maximum_fusion.block_ref
  8.3 0.0 slice-start
  8.3 47.5 %shard_map.77 = bf16[8,64,4224]{2,1,0:T(8,128)(2,1)S(1)} custom-call(bf16[64,4224]{1,0:T(8,128)(2,1)S(1)} %pad_maximum_fusion.block_ref), custom_call_target="tpu_custom_call" | custom-call | tf_op jit(solution)/shard_map/pallas_call | solution.py:193
  55.9 0.0 slice-start.1
  55.9 2.4 %fusion.7.part_ref = bf16[512,512]{1,0:T(8,128)(2,1)S(1)} fusion(bf16[512,4224]{1,0:T(8,128)(2,1)S(1)} %bitcast.15), kind=kOutput, calls=%fused_computation.5 | convolution fusion | flops 2147745792 | bytes 4718592 | tf_op jit(solution)/shard_map/dot_general | solution.py:342
  58.3 20.1 %shard_map.78 = (f32[512,512]{1,0:T(8,128)S(1)}, bf16[4,512,128]{2,1,0:T(8,128)(2,1)S(1)}) custom-call(bf16[512,512]{1,0:T(8,128)(2,1)S(1)} %fusion.7.part_ref, bf16[512,128]{1,0:T(8,128)(2,1)S(1)} %slice.37.sides_ref), custom_call_target="tpu_custom_call" | custom-call | tf_op jit(solution)/shard_map/pallas_call | solution.py:251
  78.4 0.0 slice-done
  78.4 0.0 slice-done.1
  78.4 0.0 copy-start.1
  78.4 5.9 %fusion.4 = f32[1024,512]{1,0:T(8,128)} fusion(bf16[1024,4096]{1,0:T(8,128)(2,1)S(1)} %bitcast.30, bf16[512,4224]{1,0:T(8,128)(2,1)S(1)} %bitcast.17), kind=kOutput, calls=%fused_computation.4 | convolution fusion | flops 4294967296 | bytes 14680064 | tf_op jit(solution)/shard_map/dot_general | solution.py:354
  84.3 0.0 reduce-scatter.2.cloned.1.call-update
  84.3 0.0 copy-done.1
  84.4 0.0 copy-start
  84.4 0.8 add_subtract_fusion.matrix_ref
  85.2 24.8 %shard_map.79.inverse_ref = f32[512,512]{1,0:T(8,128)S(1)} custom-call(f32[512,512]{1,0:T(8,128)S(1)} %add_subtract_fusion.matrix_ref), custom_call_target="tpu_custom_call" | custom-call | tf_op jit(solution)/shard_map/pallas_call | solution.py:114
  110.0 0.2 copy.10
  110.2 0.7 dynamic-slice_convert_fusion
  110.9 1.0 fusion.12.reduced_ref
  111.9 4.0 %reduce-scatter.2.cloned.1.call-done = f32[256,512]{1,0:T(8,128)} async-done(((f32[1024,512]{1,0:T(8,128)}), f32[256,512]{1,0:T(8,128)}) %reduce-scatter.2.cloned.1.call-update) | async-done | bytes 524304 | tf_op jit(solution)/shard_map/reduce_scatter | solution.py:357
  115.9 1.5 %multiply_subtract_fusion.rows_ref = f32[256,512]{1,0:T(8,128)S(1)} fusion(f32[256,512]{1,0:T(8,128)} %reduce-scatter.2.cloned.1.call-done, f32[512]{0:T(512)S(1)} %bitcast.26, f32[256]{0:T(256)S(1)} %bitcast.28, f32[512]{0:T(512)S(1)} %bitcast.24, f32[256]{0:T(256)S(1)} %bitcast.27), kind=kLoop, calls=%fused_computation.9 | loop fusion | flops 1441792 | bytes 1054720 | tf_op jit(solution)/shard_map/sub | solution.py:361
  117.4 0.0 copy-done
  117.4 13.4 %shard_map.80 = (f32[4,256,128]{2,1,0:T(8,128)S(1)}, f32[4,256,128]{2,1,0:T(8,128)S(1)}) custom-call(f32[256,512]{1,0:T(8,128)S(1)} %multiply_subtract_fusion.rows_ref, f32[512,512]{1,0:T(8,128)S(1)} %shard_map.79.inverse_ref, f32[512,512]{1,0:T(8,128)S(1)} %fusion.12.reduced_ref, bf16[4,256,128]{2,1,0:T(8,128)(2,1)S(1)} %bitcast.21), custom_call_target="tpu_custom_call" | custom-call | tf_op jit(solution)/shard_map/pallas_call | solution.py:321
  130.8 0.8 copy.14
  131.6 0.8 copy.15
  (5 shorter events, 0.0 us)
Async XLA Ops:
  7.2 108.7 %reduce-scatter.2.cloned.1.call-start = ((), (), s32[]{:S(2)}) async-start(), calls=%async_computation.1 | async-start | bytes 2621440 | tf_op jit(solution)/shard_map/reduce_scatter | solution.py:357
  8.3 70.1 %slice-start = ((s8[8388608]{0:T(1024)(128)(4,1)}), s8[4194304]{0:T(1024)(128)(4,1)S(1)}, s32[]{:S(2)}) async-start(s8[8388608]{0:T(1024)(128)(4,1)} %bitcast.29), calls=%async_computation.2 | async-start | bytes 8388608
  55.9 22.5 %slice-start.1 = ((s8[8388608]{0:T(1024)(128)(4,1)}), s8[4194304]{0:T(1024)(128)(4,1)S(1)}, s32[]{:S(2)}) async-start(s8[8388608]{0:T(1024)(128)(4,1)} %bitcast.29), calls=%async_computation.3 | async-start | bytes 8388608
  78.4 5.9 %copy-start.1 = (s32[2,512]{1,0:T(2,128)S(1)}, s32[2,512]{1,0:T(2,128)}, u32[]{:S(2)}) copy-start(s32[2,512]{1,0:T(2,128)} %param.7) | copy-start | bytes 12292
  84.4 33.0 %copy-start = (bf16[1024,128]{1,0:T(8,128)(2,1)S(1)}, bf16[1024,128]{1,0:T(8,128)(2,1)}, u32[]{:S(2)}) copy-start(bf16[1024,128]{1,0:T(8,128)(2,1)} %param.10) | copy-start | bytes 786436
Sparse Core Ops, SparseCore 0:
  84.4 31.4 reduce-scatter.1
